TPU v7x, 512 devices: a whole 4x4x16 slice. The times are simulated.
512 devices in a mesh: tri: 64 (over y, z), sub: 8 (over x, core).
Axes of the slice: x: 4, y: 4, z: 16, core: 2. Of those that a mesh axis runs over, the one named last changes fastest.
Arguments:
- stored_tiles: float32 [64, 10, 512, 512], P('tri', None, 'sub'), may hold values from -190 to 190, as said below
- cell_owner: int32 [64], replicated, may hold values from 0 to 63, as said below
Outputs:
- updated: float32 [64, 10, 512, 512], P('tri', None, 'sub')
Inputs may be any that keep to these rules, and one draw needn't show every extreme that they name: `cell_owner`: a permutation of the indices of tri. `stored_tiles`: every tile whose row and column blocks are equal is skew-symmetric, every pivot met is invertible, and slots that hold no tile are zero.
All inputs are finite; a program needn't handle non-finite values.
Results may differ from a plain program's by a relative error of at most 0.00035.
Values may be sent and summed in bfloat16 or wider, within the bound.
A program may use at most 64 MiB of HBM per device.

v0:
```python
import math
import jax
import jax.numpy as jnp
import numpy as np
from jax import lax
from jax.sharding import Mesh
from jax.sharding import PartitionSpec as P

NB = 32
TRI = ("tri_0", "tri_1")


def in_order(tiles, dim):
    tiles = jnp.moveaxis(tiles, 0, dim)
    dims = tiles.shape
    return tiles.reshape(*dims[:dim], dims[dim] * dims[dim + 1], *dims[dim + 2 :])


def gather_in_order(x, axes, turns):
    tiles = x[None]
    for k in turns:
        tiles = lax.all_gather(tiles, axes[k], axis=0, tiled=True)
    block = [lax.axis_size(axes[k]) for k in reversed(turns)]
    tiles = tiles.reshape(*block, *x.shape)
    turned = sorted(range(len(turns)), key=lambda place: turns[len(turns) - 1 - place])
    return tiles.transpose(*turned, *range(len(turns), tiles.ndim)).reshape(-1, *x.shape)


def gather_axes(x, axes, turns, dim):
    return in_order(gather_in_order(x, axes, turns), dim)


def layout(groups, per_group):
    half_group = per_group // 2
    slot_count = per_group * (per_group + 1) // 2
    row_table = np.full((groups * groups, slot_count), -1, np.int32)
    col_table = np.full((groups * groups, slot_count), -1, np.int32)
    for first_group in range(groups):
        for second_group in range(groups):
            cell_index = first_group * groups + second_group
            for inner_row in range(per_group):
                if first_group == second_group:
                    for inner_column in range(inner_row + 1):
                        slot_index = inner_row * (inner_row + 1) // 2 + inner_column
                        row_table[cell_index, slot_index] = first_group * per_group + inner_row
                        col_table[cell_index, slot_index] = first_group * per_group + inner_column
                else:
                    for inner_column in range(half_group):
                        slot_index = inner_row * half_group + inner_column
                        if first_group > second_group:
                            row_table[cell_index, slot_index] = first_group * per_group + inner_row
                            col_table[cell_index, slot_index] = (
                                second_group * per_group + inner_column
                            )
                        else:
                            row_table[cell_index, slot_index] = second_group * per_group + inner_row
                            col_table[cell_index, slot_index] = (
                                first_group * per_group + half_group + inner_column
                            )
    return (row_table, col_table)


def shards(stored_tiles, cell_owner):
    tri_count = lax.axis_size(TRI)
    groups = math.isqrt(tri_count)
    per_group = NB // groups
    half_group = per_group // 2
    strip_rows = stored_tiles.shape[2]
    block_order = stored_tiles.shape[3]
    row_table, col_table = layout(groups, per_group)
    position = lax.axis_index(TRI)
    my_cell = jnp.sum(jnp.where(cell_owner == position, jnp.arange(tri_count, dtype=jnp.int32), 0))
    cell_down = my_cell // groups
    cell_across = my_cell % groups
    row_group = jnp.maximum(cell_down, cell_across)
    col_group = jnp.minimum(cell_down, cell_across)
    my_rows = jnp.asarray(row_table)[my_cell]
    my_cols = jnp.asarray(col_table)[my_cell]
    row_local = jnp.clip(my_rows - row_group * per_group, 0, per_group - 1)
    col_local = jnp.clip(my_cols - col_group * per_group, 0, per_group - 1)
    holders = cell_owner[jnp.arange(groups) * groups]
    highest = lax.Precision.HIGHEST
    current = stored_tiles[0]
    lower_slots = np.array([member * half_group for member in range(per_group)], np.int32)
    first_slots = np.array(
        [member * (member + 1) // 2 if member > 0 else 0 for member in range(per_group)], np.int32
    )
    keep_first = np.array([1.0 if member > 0 else 0.0 for member in range(per_group)], np.float32)
    from_lower = current[lower_slots]
    from_first = current[first_slots] * keep_first[:, None, None]
    holder_part = jnp.where(cell_down > 0, from_lower, from_first)
    holder_part = jnp.where(cell_across == 0, holder_part, 0.0).astype(jnp.bfloat16)
    pivot_slot = 0 // 2
    pivot_part = jnp.where(my_cell == 0, current[pivot_slot], 0.0)
    piece_size = holder_part.size // tri_count
    spread_panel = lax.all_to_all(
        holder_part.reshape(tri_count, piece_size), TRI, split_axis=0, concat_axis=0, tiled=True
    )
    spread_pivot = lax.all_to_all(
        pivot_part.astype(jnp.bfloat16), TRI, split_axis=0, concat_axis=0, tiled=True
    ).astype(pivot_part.dtype)
    picked_panel = spread_panel[holders][:, None, :]
    picked_pivot = spread_pivot[holders[0]][None, :]
    whole_panel = gather_axes(picked_panel, TRI, (0, 1), 1)
    whole_pivot = gather_axes(picked_pivot.astype(jnp.bfloat16), TRI, (0, 1), 0).astype(
        picked_pivot.dtype
    )
    panels = whole_panel.reshape(groups, per_group, strip_rows, block_order)
    own_strips = panels[row_group]
    other_strips = panels[col_group]
    pivot_block = lax.all_gather(
        whole_pivot.astype(jnp.bfloat16), "sub", axis=0, tiled=True
    ).astype(whole_pivot.dtype)
    partner = lax.all_gather(other_strips, "sub", axis=1, tiled=True)
    gram_matrix = jnp.dot(pivot_block.T, pivot_block, precision=highest)
    factor = jnp.linalg.cholesky(gram_matrix)
    inverse = jax.scipy.linalg.cho_solve((factor, True), pivot_block.T)
    scaled = jnp.einsum(
        "irk,kc->irc", own_strips.astype(jnp.float32), inverse, precision=highest
    ).astype(jnp.bfloat16)
    left_slots = scaled[row_local]
    right_slots = partner[col_local]
    update = jnp.einsum("qrk,qck->qrc", left_slots, right_slots, preferred_element_type=jnp.float32)
    live_slots = (my_rows > 0) & (my_cols > 0)
    current = current + jnp.where(live_slots[:, None, None], update, 0.0)
    return current[None]


def solution(mesh):
    torus = Mesh(mesh.devices.reshape(4, 16, mesh.shape["sub"]), ("tri_0", "tri_1", "sub"))
    return jax.shard_map(
        shards,
        mesh=torus,
        in_specs=(P(TRI, None, "sub", None), P()),
        out_specs=P(TRI, None, "sub", None),
        check_vma=False,
    )
```

profile of v0, /device:TPU:1, one launch (start us, length us, event | category | flops | bytes accessed | tf_op | source)
XLA Modules:
  0.0 323.7 jit_solution(5538113034983923474)
XLA Ops:
  6.5 1.4 fusion.56
  8.6 0.9 fusion.39
  10.6 0.6 reshape.305
  11.3 19.3 %all-to-all-start.1 = ((bf16[64,2,256]{2,1,0:T(2,128)(2,1)}), bf16[64,2,256]{2,1,0:T(2,128)(2,1)S(1)}, u32[]{:S(2)}, u32[]{:S(2)}) async-start(bf16[64,2,256]{2,1,0:T(2,128)(2,1)} %reshape.305), calls=%async_computation.1 | async-start | bytes 131072 | tf_op jit(solution)/shard_map/all_to_all | solution.py:99
  33.4 1.3 gather_fusion.2
  34.7 0.7 pad_clamp_fusion.4
  35.4 1.9 gather_fusion.1
  37.3 1.9 gather_fusion
  40.6 0.7 fusion.59
  41.3 0.7 and_bitcast_fusion
  42.2 0.7 fusion.60
  43.2 2.1 reduce.26
  45.2 0.9 reshape.307
  46.2 14.6 %all-to-all-start = ((bf16[64,2,1024]{2,1,0:T(2,128)(2,1)}), bf16[64,2,1024]{2,1,0:T(2,128)(2,1)S(1)}, u32[]{:S(2)}, u32[]{:S(2)}) async-start(bf16[64,2,1024]{2,1,0:T(2,128)(2,1)} %reshape.307), calls=%async_computation | async-start | bytes 524288 | tf_op jit(solution)/shard_map/all_to_all | solution.py:96
  60.9 8.8 %all_gather.20 = bf16[4,1,512]{2,1,0:T(2,128)(2,1)S(1)} all-gather(bf16[1,1,512]{2,1,0:T(2,128)(2,1)S(1)} %fusion.54), channel_id=1, replica_groups=mesh['tri_0'=4,'tri_1'=16,'sub'=8] {'tri_0'}, dimensions={0}, use_global_device_ids=true | all-gather | bytes 5120 | tf_op jit(solution)/shard_map/all_gather | solution.py:22
  69.7 23.8 %all_gather.21 = bf16[64,1,512]{2,1,0:T(2,128)(2,1)S(1)} all-gather(bf16[4,1,512]{2,1,0:T(2,128)(2,1)S(1)} %all_gather.20), channel_id=1, replica_groups=mesh['tri_0'=4,'tri_1'=16,'sub'=8] {'tri_1'}, dimensions={0}, use_global_device_ids=true | all-gather | bytes 69632 | tf_op jit(solution)/shard_map/all_gather | solution.py:22
  93.9 23.9 %all_gather.22 = bf16[512,512]{1,0:T(8,128)(2,1)S(1)} all-gather(bf16[64,512]{1,0:T(8,128)(2,1)S(1)} %bitcast.120), channel_id=1, replica_groups=mesh['tri_0'=4,'tri_1'=16,'sub'=8] {'sub'}, dimensions={0}, use_global_device_ids=true | all-gather | bytes 589824 | tf_op jit(solution)/shard_map/all_gather | solution.py:111
  118.9 1.0 copy-done.1
  119.9 11.7 %cholesky.104 = f32[128,128]{1,0:T(8,128)S(1)} custom-call(f32[128,128]{1,0:T(8,128)S(1)} %cholesky.266), custom_call_target="Cholesky" | custom-call | tf_op jit(solution)/shard_map/jit(cholesky)/cholesky | solution.py:116
  131.6 9.8 %custom-call.34 = f32[1,128,128]{1,2,0:T(8,128)S(1)} custom-call(f32[1,128,128]{2,1,0:T(8,128)S(1)} %get-tuple-element.32), custom_call_target="InvertDiagBlocksLowerTriangular" | custom-call | tf_op jit(solution)/shard_map/jit(cholesky)/cholesky | solution.py:116
  142.6 9.8 %all-gather = bf16[32,2048]{1,0:T(8,128)(2,1)} all-gather(bf16[8,2048]{1,0:T(8,128)(2,1)S(1)} %gather_fusion.3), channel_id=2, replica_groups=mesh['tri_0'=4,'tri_1'=16,'sub'=8] {'tri_0'}, dimensions={0}, use_global_device_ids=true | all-gather | bytes 163840 | tf_op jit(solution)/shard_map/all_gather | solution.py:22
  153.0 1.0 copy.32
  154.3 11.7 %cholesky.217 = f32[128,128]{1,0:T(8,128)S(1)} custom-call(f32[128,128]{1,0:T(8,128)S(1)} %cholesky.270), custom_call_target="Cholesky" | custom-call | tf_op jit(solution)/shard_map/jit(cholesky)/cholesky | solution.py:116
  166.1 9.8 %custom-call.35 = f32[1,128,128]{1,2,0:T(8,128)S(1)} custom-call(f32[1,128,128]{2,1,0:T(8,128)S(1)} %get-tuple-element.29), custom_call_target="InvertDiagBlocksLowerTriangular" | custom-call | tf_op jit(solution)/shard_map/jit(cholesky)/cholesky | solution.py:116
  176.6 11.7 %cholesky.238 = f32[128,128]{1,0:T(8,128)S(1)} custom-call(f32[128,128]{1,0:T(8,128)S(1)} %cholesky.275), custom_call_target="Cholesky" | custom-call | tf_op jit(solution)/shard_map/jit(cholesky)/cholesky | solution.py:116
  188.3 10.0 %custom-call.36 = f32[1,128,128]{1,2,0:T(8,128)S(1)} custom-call(f32[1,128,128]{2,1,0:T(8,128)S(1)} %get-tuple-element.26), custom_call_target="InvertDiagBlocksLowerTriangular" | custom-call | tf_op jit(solution)/shard_map/jit(cholesky)/cholesky | solution.py:116
  198.9 11.7 %cholesky.255 = f32[128,128]{1,0:T(8,128)S(1)} custom-call(f32[128,128]{1,0:T(8,128)S(1)} %convolution_subtract_fusion.8), custom_call_target="Cholesky" | custom-call | tf_op jit(solution)/shard_map/jit(cholesky)/cholesky | solution.py:116
  210.6 0.7 compare_reduce_fusion.2
  212.7 0.7 compare_reduce_fusion.1
  214.1 0.7 compare_reduce_fusion
  215.7 10.8 %while.1 = (s32[]{:T(128)}, f32[512,512]{1,0:T(8,128)S(1)}, s32[4,2]{0,1:T(2,128)S(1)}, f32[4,128,128]{2,1,0:T(8,128)}, s32[]{:T(128)}) while((s32[]{:T(128)}, f32[512,512]{1,0:T(8,128)S(1)}, s32[4,2]{0,1:T(2,128)S(1)}, f32[4,128,128]{2,1,0:T(8,128)}, s32[]{:T(128)}) %tuple.27), condition=%wide.while_cond, body=%wide.while_body.sunk | while | flops 2 | bytes 132705 | solution.py:117
  216.4 2.0 bitcast_dynamic-update-slice_fusion.2
  219.1 2.0 bitcast_dynamic-update-slice_fusion.2
  221.8 2.0 bitcast_dynamic-update-slice_fusion.2
  224.5 2.0 bitcast_dynamic-update-slice_fusion.2
  226.5 40.1 %custom-call.37 = f32[4,128,128]{1,2,0:T(8,128)S(1)} custom-call(f32[4,128,128]{2,1,0:T(8,128)} %get-tuple-element.12), custom_call_target="InvertDiagBlocksLowerTriangular" | custom-call | tf_op jit(solution)/shard_map/jit(_cho_solve)/triangular_solve | solution.py:117
  266.7 1.7 copy.27
  268.4 1.2 copy.28
  269.6 2.6 reshape_reshape.6
  272.2 1.7 constant_dynamic-slice_fusion.1
  273.9 1.2 fusion.35
  275.1 1.2 bitcast_convert_fusion
  278.0 0.6 convolution_subtract_fusion.5
  281.0 0.7 convolution_subtract_fusion.4
  282.1 1.6 convolution_convert_fusion
  284.3 21.5 %all-gather.7.cloned.1.call-done = bf16[1,4,512,512]{3,2,1,0:T(8,128)(2,1)} async-done(((bf16[1,4,64,512]{3,2,1,0:T(8,128)(2,1)}), bf16[1,4,512,512]{3,2,1,0:T(8,128)(2,1)}) %all-gather.7.cloned.1.call-update) | async-done | bytes 2097168 | tf_op jit(solution)/shard_map/all_gather | solution.py:114
  305.8 5.5 %gather_fusion.5 = bf16[10,512,512]{2,1,0:T(8,128)(2,1)} fusion(bf16[4,512,512]{2,1,0:T(8,128)(2,1)} %bitcast.112, s32[1024]{0:T(1024)S(1)} %pad_clamp_fusion), kind=kCustom, calls=%fused_computation.5 | custom fusion | bytes 10485800 | tf_op jit(solution)/shard_map/gather | solution.py:122
  311.4 5.2 %fusion.1 = f32[1,10,64,512]{3,2,1,0:T(8,128)} fusion(bf16[10,64,512]{2,1,0:T(8,128)(2,1)S(1)} %gather_fusion.4, bf16[10,512,512]{2,1,0:T(8,128)(2,1)} %gather_fusion.5, pred[10]{0:T(512)(128)(4,1)S(1)} %and_bitcast_fusion, f32[1,10,64,512]{3,2,1,0:T(8,128)S(1)} %copy-done), kind=kOutput, calls=%fused_computation.10 | convolution fusion | flops 336199680 | bytes 8519690 | tf_op jit(solution)/shard_map/qrk,qck->qrc/dot_general | solution.py:123
  (75 shorter events, 14.2 us)
Async XLA Ops:
  6.5 35.5 %copy-start.3 = (f32[4]{0:T(128)S(1)}, f32[4]{0:T(128)}, u32[]{:S(2)}) copy-start(f32[4]{0:T(128)} %constant.245) | copy-start | bytes 52
  11.3 34.9 %all-to-all-start.1 = ((bf16[64,2,256]{2,1,0:T(2,128)(2,1)}), bf16[64,2,256]{2,1,0:T(2,128)(2,1)S(1)}, u32[]{:S(2)}, u32[]{:S(2)}) async-start(bf16[64,2,256]{2,1,0:T(2,128)(2,1)} %reshape.305), calls=%async_computation.1 | async-start | bytes 131072 | tf_op jit(solution)/shard_map/all_to_all | solution.py:99
  46.2 95.4 %all-to-all-start = ((bf16[64,2,1024]{2,1,0:T(2,128)(2,1)}), bf16[64,2,1024]{2,1,0:T(2,128)(2,1)S(1)}, u32[]{:S(2)}, u32[]{:S(2)}) async-start(bf16[64,2,1024]{2,1,0:T(2,128)(2,1)} %reshape.307), calls=%async_computation | async-start | bytes 524288 | tf_op jit(solution)/shard_map/all_to_all | solution.py:96
  60.8 205.9 %all-gather.5.cloned.1.call-start = ((), (), s32[]{:S(2)}) async-start(), calls=%async_computation.2 | async-start | bytes 2228224 | tf_op jit(solution)/shard_map/all_gather | solution.py:22
  118.9 1.0 copy-start.1
  119.9 32.8 %copy-start.2 = (f32[512,512]{1,0:T(8,128)S(1)}, f32[512,512]{1,0:T(8,128)}, u32[]{:S(2)}) copy-start(f32[512,512]{1,0:T(8,128)} %copy-done.1) | copy-start | bytes 3145732
  152.4 153.4 %all-gather.7.cloned.1.call-start = ((), (), s32[]{:S(2)}) async-start(), calls=%async_computation.3 | async-start | bytes 2359296 | tf_op jit(solution)/shard_map/all_gather | solution.py:114
  305.8 5.6 %copy-start = (f32[1,10,64,512]{3,2,1,0:T(8,128)S(1)}, f32[1,10,64,512]{3,2,1,0:T(8,128)}, u32[]{:S(2)}) copy-start(f32[1,10,64,512]{3,2,1,0:T(8,128)} %param.9) | copy-start | bytes 3932164
Sparse Core Ops, SparseCore 0:
  152.6 63.2 all-gather.4
  274.0 31.7 all-gather.6
where the time goes:
time: 329 us; the launch traced here: 324 us
  other arithmetic  129 us (39%)
  blocking collectives  66.3 us (20%)
  local copies, waits for them, and re-layouts  34.9 us (11%)
  starting transfers between devices  34.1 us (10%)
  between operations  21.9 us (7%)
  waiting for transfers between devices  21.6 us (7%)
  matrix products  16.1 us (5%)
    another operation x14, other arithmetic, shards(): factor = jnp.linalg.cholesky(gram_matrix)  78.8 us
    all_gather x3, blocking collectives, gather_in_order(): tiles = lax.all_gather(tiles, axes[k], axis=0, tiled=True)  42.5 us
    another operation x3, other arithmetic, shards(): inverse = jax.scipy.linalg.cho_solve((factor, True), pivot_block.T)  40.3 us
    all_gather x1, blocking collectives, shards(): lax.all_gather(whole_pivot.astype(jnp.bfloat16), 'sub', axis=0, tiled=True)  23.9 us
    all_gather x1, waiting for transfers between devices, shards(): partner = lax.all_gather(other_strips, 'sub', axis=1, tiled=True)  21.5 us
    all_to_all x1, starting transfers between devices, shards(): lax.all_to_all(pivot_part.astype(jnp.bfloat16), TRI, split_axis=0, concat...  19.3 us
    all_to_all x1, starting transfers between devices, shards(): lax.all_to_all(holder_part.reshape(tri_count, piece_size), TRI, split_axi...  14.6 us
    another operation x12, local copies, waits for them, and re-layouts  10.8 us
  transfers between devices with their start and end apart: 4, of which 1 were waited for; matrix products, arithmetic and copies ran while one was open for 48% of the time, Pallas kernels for 0%

commit v1 on v0

--- a/solution.py
+++ b/solution.py
@@ -8,6 +8,16 @@
 
 NB = 32
 TRI = ("tri_0", "tri_1")
+
+
+def turned_line(block, axis, dim):
+    n_dev = lax.axis_size(axis)
+    moving, blocks = (block, [block])
+    for _ in range(n_dev - 1):
+        moving = lax.ppermute(moving, axis, [(i, (i + 1) % n_dev) for i in range(n_dev)])
+        blocks.insert(0, moving)
+    line = jnp.concatenate(blocks, axis=dim)
+    return jnp.roll(line, (lax.axis_index(axis) + 1) * block.shape[dim], axis=dim)
 
 
 def in_order(tiles, dim):
@@ -111,7 +121,7 @@
     pivot_block = lax.all_gather(
         whole_pivot.astype(jnp.bfloat16), "sub", axis=0, tiled=True
     ).astype(whole_pivot.dtype)
-    partner = lax.all_gather(other_strips, "sub", axis=1, tiled=True)
+    partner = turned_line(other_strips, "sub", 1)
     gram_matrix = jnp.dot(pivot_block.T, pivot_block, precision=highest)
     factor = jnp.linalg.cholesky(gram_matrix)
     inverse = jax.scipy.linalg.cho_solve((factor, True), pivot_block.T)

time: 329 us -> 348 us (1.058)
  the two profiles are of different devices: /device:TPU:1 before, /device:TPU:8 now
where the time goes in v1:
time: 348 us; the launch traced here: 343 us
  other arithmetic  130 us (37%)
  blocking collectives  67 us (19%)
  waiting for transfers between devices  35.6 us (10%)
  local copies, waits for them, and re-layouts  33.9 us (10%)
  starting transfers between devices  33.9 us (10%)
  between operations  21.6 us (6%)
  matrix products  20.8 us (6%)
    another operation x15, other arithmetic, shards(): factor = jnp.linalg.cholesky(gram_matrix)  79.1 us
    all_gather x3, blocking collectives, gather_in_order(): tiles = lax.all_gather(tiles, axes[k], axis=0, tiled=True)  53 us
    another operation x3, other arithmetic, shards(): inverse = jax.scipy.linalg.cho_solve((factor, True), pivot_block.T)  40.3 us
    ppermute x7, waiting for transfers between devices, turned_line(): lax.ppermute(moving, axis, [(i, (i + 1) % n_dev) for i in range(n_dev)])  35.6 us
    all_to_all x1, starting transfers between devices, shards(): lax.all_to_all(pivot_part.astype(jnp.bfloat16), TRI, split_axis=0, concat...  18.7 us
    all_to_all x1, starting transfers between devices, shards(): lax.all_to_all(holder_part.reshape(tri_count, piece_size), TRI, split_axi...  15.1 us
    all_gather x1, blocking collectives, shards(): lax.all_gather(whole_pivot.astype(jnp.bfloat16), 'sub', axis=0, tiled=True)  13.9 us
    another operation x14, matrix products, shards(): inverse = jax.scipy.linalg.cho_solve((factor, True), pivot_block.T)  10.5 us
  transfers between devices with their start and end apart: 10, of which 7 were waited for; matrix products, arithmetic and copies ran while one was open for 47% of the time, Pallas kernels for 0%

profile of v1, /device:TPU:8, one launch (start us, length us, event | category | flops | bytes accessed | tf_op | source)
XLA Modules:
  0.0 342.7 jit_solution(9222917224167894235)
XLA Ops:
  6.5 1.4 fusion.56
  11.3 18.7 %all-to-all-start.1 = ((bf16[64,2,256]{2,1,0:T(2,128)(2,1)}), bf16[64,2,256]{2,1,0:T(2,128)(2,1)S(1)}, u32[]{:S(2)}, u32[]{:S(2)}) async-start(bf16[64,2,256]{2,1,0:T(2,128)(2,1)} %reshape.304), calls=%async_computation.1 | async-start | bytes 131072 | tf_op jit(solution)/shard_map/all_to_all | solution.py:109
  33.5 1.9 gather_fusion.1
  35.4 1.9 gather_fusion
  37.3 1.3 gather_fusion.2
  43.2 2.1 reduce.26
  46.3 15.1 %all-to-all-start = ((bf16[64,2,1024]{2,1,0:T(2,128)(2,1)}), bf16[64,2,1024]{2,1,0:T(2,128)(2,1)S(1)}, u32[]{:S(2)}, u32[]{:S(2)}) async-start(bf16[64,2,1024]{2,1,0:T(2,128)(2,1)} %reshape.306), calls=%async_computation | async-start | bytes 524288 | tf_op jit(solution)/shard_map/all_to_all | solution.py:106
  61.5 10.9 %all_gather.17 = bf16[4,1,512]{2,1,0:T(2,128)(2,1)S(1)} all-gather(bf16[1,1,512]{2,1,0:T(2,128)(2,1)S(1)} %fusion.54), channel_id=1, replica_groups=mesh['tri_0'=4,'tri_1'=16,'sub'=8] {'tri_0'}, dimensions={0}, use_global_device_ids=true | all-gather | bytes 5120 | tf_op jit(solution)/shard_map/all_gather | solution.py:32
  72.5 29.9 %all_gather.18 = bf16[64,1,512]{2,1,0:T(2,128)(2,1)S(1)} all-gather(bf16[4,1,512]{2,1,0:T(2,128)(2,1)S(1)} %all_gather.17), channel_id=1, replica_groups=mesh['tri_0'=4,'tri_1'=16,'sub'=8] {'tri_1'}, dimensions={0}, use_global_device_ids=true | all-gather | bytes 69632 | tf_op jit(solution)/shard_map/all_gather | solution.py:32
  102.8 13.9 %all_gather.19 = bf16[512,512]{1,0:T(8,128)(2,1)S(1)} all-gather(bf16[64,512]{1,0:T(8,128)(2,1)S(1)} %bitcast.124), channel_id=1, replica_groups=mesh['tri_0'=4,'tri_1'=16,'sub'=8] {'sub'}, dimensions={0}, use_global_device_ids=true | all-gather | bytes 589824 | tf_op jit(solution)/shard_map/all_gather | solution.py:121
  117.2 1.0 copy.32
  118.8 11.7 %cholesky.104 = f32[128,128]{1,0:T(8,128)S(1)} custom-call(f32[128,128]{1,0:T(8,128)S(1)} %cholesky.266), custom_call_target="Cholesky" | custom-call | tf_op jit(solution)/shard_map/jit(cholesky)/cholesky | solution.py:126
  130.5 9.8 %custom-call.34 = f32[1,128,128]{1,2,0:T(8,128)S(1)} custom-call(f32[1,128,128]{2,1,0:T(8,128)S(1)} %get-tuple-element.32), custom_call_target="InvertDiagBlocksLowerTriangular" | custom-call | tf_op jit(solution)/shard_map/jit(cholesky)/cholesky | solution.py:126
  141.2 11.7 %cholesky.217 = f32[128,128]{1,0:T(8,128)S(1)} custom-call(f32[128,128]{1,0:T(8,128)S(1)} %cholesky.270), custom_call_target="Cholesky" | custom-call | tf_op jit(solution)/shard_map/jit(cholesky)/cholesky | solution.py:126
  152.9 9.9 %custom-call.35 = f32[1,128,128]{1,2,0:T(8,128)S(1)} custom-call(f32[1,128,128]{2,1,0:T(8,128)S(1)} %get-tuple-element.29), custom_call_target="InvertDiagBlocksLowerTriangular" | custom-call | tf_op jit(solution)/shard_map/jit(cholesky)/cholesky | solution.py:126
  163.9 12.2 %all-gather = bf16[32,2048]{1,0:T(8,128)(2,1)} all-gather(bf16[8,2048]{1,0:T(8,128)(2,1)S(1)} %gather_fusion.3), channel_id=2, replica_groups=mesh['tri_0'=4,'tri_1'=16,'sub'=8] {'tri_0'}, dimensions={0}, use_global_device_ids=true | all-gather | bytes 163840 | tf_op jit(solution)/shard_map/all_gather | solution.py:32
  176.1 1.2 convolution_dynamic-update-slice_fusion
  177.7 11.7 %cholesky.238 = f32[128,128]{1,0:T(8,128)S(1)} custom-call(f32[128,128]{1,0:T(8,128)S(1)} %cholesky.275), custom_call_target="Cholesky" | custom-call | tf_op jit(solution)/shard_map/jit(cholesky)/cholesky | solution.py:126
  189.4 9.8 %custom-call.36 = f32[1,128,128]{1,2,0:T(8,128)S(1)} custom-call(f32[1,128,128]{2,1,0:T(8,128)S(1)} %get-tuple-element.26), custom_call_target="InvertDiagBlocksLowerTriangular" | custom-call | tf_op jit(solution)/shard_map/jit(cholesky)/cholesky | solution.py:126
  199.8 11.7 %cholesky.255 = f32[128,128]{1,0:T(8,128)S(1)} custom-call(f32[128,128]{1,0:T(8,128)S(1)} %convolution_subtract_fusion.8), custom_call_target="Cholesky" | custom-call | tf_op jit(solution)/shard_map/jit(cholesky)/cholesky | solution.py:126
  216.6 10.2 %while.1 = (s32[]{:T(128)}, f32[512,512]{1,0:T(8,128)S(1)}, s32[4,2]{0,1:T(2,128)S(1)}, f32[4,128,128]{2,1,0:T(8,128)}, s32[]{:T(128)}) while((s32[]{:T(128)}, f32[512,512]{1,0:T(8,128)S(1)}, s32[4,2]{0,1:T(2,128)S(1)}, f32[4,128,128]{2,1,0:T(8,128)}, s32[]{:T(128)}) %tuple.28), condition=%wide.while_cond, body=%wide.while_body.sunk | while | flops 2 | bytes 132705 | solution.py:127
  217.4 1.9 bitcast_dynamic-update-slice_fusion.2
  219.9 1.9 bitcast_dynamic-update-slice_fusion.2
  222.4 1.9 bitcast_dynamic-update-slice_fusion.2
  224.9 1.9 bitcast_dynamic-update-slice_fusion.2
  226.8 40.1 %custom-call.37 = f32[4,128,128]{1,2,0:T(8,128)S(1)} custom-call(f32[4,128,128]{2,1,0:T(8,128)} %get-tuple-element.12), custom_call_target="InvertDiagBlocksLowerTriangular" | custom-call | tf_op jit(solution)/shard_map/jit(_cho_solve)/triangular_solve | solution.py:127
  267.3 1.1 bitcast_convert_fusion
  268.4 1.7 copy.27
  270.1 1.2 copy.28
  271.3 2.6 reshape_reshape.6
  273.9 1.0 dynamic-slice_bitcast_fusion
  274.9 1.3 convolution_subtract_fusion.3
  276.2 1.3 fusion.49
  277.5 4.4 %collective-permute-done = bf16[4,64,512]{2,1,0:T(8,128)(2,1)S(1)} collective-permute-done((bf16[4,64,512]{2,1,0:T(8,128)(2,1)S(1)}, bf16[4,64,512]{2,1,0:T(8,128)(2,1)S(1)}, u32[]{:S(2)}, u32[]{:S(2)}) %collective-permute-start) | collective-permute-done | bytes 262176 | tf_op jit(solution)/shard_map/ppermute | solution.py:17
  281.9 1.4 convolution_subtract_fusion.2
  283.3 1.3 fusion.51
  284.5 4.4 %collective-permute-done.1 = bf16[4,64,512]{2,1,0:T(8,128)(2,1)S(1)} collective-permute-done((bf16[4,64,512]{2,1,0:T(8,128)(2,1)S(1)}, bf16[4,64,512]{2,1,0:T(8,128)(2,1)S(1)}, u32[]{:S(2)}, u32[]{:S(2)}) %collective-permute-start.1) | collective-permute-done | bytes 262176 | tf_op jit(solution)/shard_map/ppermute | solution.py:17
  288.9 1.6 convolution_subtract_fusion.5
  290.9 5.0 %collective-permute-done.2 = bf16[4,64,512]{2,1,0:T(8,128)(2,1)S(1)} collective-permute-done((bf16[4,64,512]{2,1,0:T(8,128)(2,1)S(1)}, bf16[4,64,512]{2,1,0:T(8,128)(2,1)S(1)}, u32[]{:S(2)}, u32[]{:S(2)}) %collective-permute-start.2) | collective-permute-done | bytes 262176 | tf_op jit(solution)/shard_map/ppermute | solution.py:17
  296.7 6.2 %collective-permute-done.3 = bf16[4,64,512]{2,1,0:T(8,128)(2,1)S(1)} collective-permute-done((bf16[4,64,512]{2,1,0:T(8,128)(2,1)S(1)}, bf16[4,64,512]{2,1,0:T(8,128)(2,1)S(1)}, u32[]{:S(2)}, u32[]{:S(2)}) %collective-permute-start.3) | collective-permute-done | bytes 262176 | tf_op jit(solution)/shard_map/ppermute | solution.py:17
  303.8 6.2 %collective-permute-done.4 = bf16[4,64,512]{2,1,0:T(8,128)(2,1)S(1)} collective-permute-done((bf16[4,64,512]{2,1,0:T(8,128)(2,1)S(1)}, bf16[4,64,512]{2,1,0:T(8,128)(2,1)S(1)}, u32[]{:S(2)}, u32[]{:S(2)}) %collective-permute-start.4) | collective-permute-done | bytes 262176 | tf_op jit(solution)/shard_map/ppermute | solution.py:17
  311.0 6.0 %collective-permute-done.5 = bf16[4,64,512]{2,1,0:T(8,128)(2,1)S(1)} collective-permute-done((bf16[4,64,512]{2,1,0:T(8,128)(2,1)S(1)}, bf16[4,64,512]{2,1,0:T(8,128)(2,1)S(1)}, u32[]{:S(2)}, u32[]{:S(2)}) %collective-permute-start.5) | collective-permute-done | bytes 262176 | tf_op jit(solution)/shard_map/ppermute | solution.py:17
  317.3 1.6 convolution_convert_fusion
  318.9 1.5 gather_fusion.4
  320.4 3.5 %collective-permute-done.6 = bf16[4,64,512]{2,1,0:T(8,128)(2,1)S(1)} collective-permute-done((bf16[4,64,512]{2,1,0:T(8,128)(2,1)S(1)}, bf16[4,64,512]{2,1,0:T(8,128)(2,1)S(1)}, u32[]{:S(2)}, u32[]{:S(2)}) %collective-permute-start.6) | collective-permute-done | bytes 262176 | tf_op jit(solution)/shard_map/ppermute | solution.py:17
  324.1 1.0 constant_dynamic-update-slice_fusion.8
  326.4 3.7 %gather_fusion.5 = bf16[10,512,512]{2,1,0:T(8,128)(2,1)} fusion(bf16[4,512,512]{2,1,0:T(8,128)(2,1)S(1)} %constant_dynamic-slice_fusion.1, s32[1024]{0:T(1024)S(1)} %get-tuple-element.35), kind=kCustom, calls=%fused_computation.5 | custom fusion | bytes 10485800 | tf_op jit(solution)/shard_map/gather | solution.py:132
  330.2 5.4 %fusion.1 = f32[1,10,64,512]{3,2,1,0:T(8,128)} fusion(bf16[10,64,512]{2,1,0:T(8,128)(2,1)} %gather_fusion.4, bf16[10,512,512]{2,1,0:T(8,128)(2,1)} %gather_fusion.5, pred[10]{0:T(512)(128)(4,1)S(1)} %and_bitcast_fusion, f32[1,10,64,512]{3,2,1,0:T(8,128)S(1)} %copy-done), kind=kOutput, calls=%fused_computation.10 | convolution fusion | flops 336199680 | bytes 8519690 | tf_op jit(solution)/shard_map/qrk,qck->qrc/dot_general | solution.py:133
  (104 shorter events, 22.0 us)
Async XLA Ops:
  11.3 35.0 %all-to-all-start.1 = ((bf16[64,2,256]{2,1,0:T(2,128)(2,1)}), bf16[64,2,256]{2,1,0:T(2,128)(2,1)S(1)}, u32[]{:S(2)}, u32[]{:S(2)}) async-start(bf16[64,2,256]{2,1,0:T(2,128)(2,1)} %reshape.304), calls=%async_computation.1 | async-start | bytes 131072 | tf_op jit(solution)/shard_map/all_to_all | solution.py:109
  46.3 116.6 %all-to-all-start = ((bf16[64,2,1024]{2,1,0:T(2,128)(2,1)}), bf16[64,2,1024]{2,1,0:T(2,128)(2,1)S(1)}, u32[]{:S(2)}, u32[]{:S(2)}) async-start(bf16[64,2,1024]{2,1,0:T(2,128)(2,1)} %reshape.306), calls=%async_computation | async-start | bytes 524288 | tf_op jit(solution)/shard_map/all_to_all | solution.py:106
  61.4 206.9 %all-gather.3.cloned.1.call-start = ((), (), s32[]{:S(2)}) async-start(), calls=%async_computation.2 | async-start | bytes 2228224 | tf_op jit(solution)/shard_map/all_gather | solution.py:32
  140.8 126.1 %copy-start.1 = (bf16[512,512]{0,1:T(8,128)(2,1)S(1)}, bf16[512,512]{0,1:T(8,128)(2,1)}, u32[]{:S(2)}) copy-start(bf16[512,512]{0,1:T(8,128)(2,1)} %copy.32) | copy-start | bytes 1572868
  141.1 21.7 %copy-start.4 = (f32[384,128]{1,0:T(8,128)}, f32[384,128]{1,0:T(8,128)S(1)}, u32[]{:S(2)}) copy-start(f32[384,128]{1,0:T(8,128)S(1)} %convolution_subtract_fusion.6) | copy-start | bytes 589828
  266.9 3.2 copy-start.2
  273.9 16.6 %copy-start.3 = (f32[4,128,128]{1,2,0:T(8,128)S(1)}, f32[4,128,128]{1,2,0:T(8,128)}, u32[]{:S(2)}) copy-start(f32[4,128,128]{1,2,0:T(8,128)} %copy-done.2) | copy-start | bytes 786436
  274.9 7.0 %collective-permute-start = (bf16[4,64,512]{2,1,0:T(8,128)(2,1)S(1)}, bf16[4,64,512]{2,1,0:T(8,128)(2,1)S(1)}, u32[]{:S(2)}, u32[]{:S(2)}) collective-permute-start(bf16[4,64,512]{2,1,0:T(8,128)(2,1)S(1)} %dynamic-slice_bitcast_fusion), channel_id=1, source_target_pairs={{0,1},{1,2},{2,3},{3,4},{4,5},{5,6},{6,7},{7,0},{8,9},{9,10},{10,1... | collective-permute-start | bytes 786440 | tf_op jit(solution)/shard_map/ppermute | solution.py:17
  281.9 7.0 %collective-permute-start.1 = (bf16[4,64,512]{2,1,0:T(8,128)(2,1)S(1)}, bf16[4,64,512]{2,1,0:T(8,128)(2,1)S(1)}, u32[]{:S(2)}, u32[]{:S(2)}) collective-permute-start(bf16[4,64,512]{2,1,0:T(8,128)(2,1)S(1)} %collective-permute-done), channel_id=1, source_target_pairs={{0,1},{1,2},{2,3},{3,4},{4,5},{5,6},{6,7},{7,0},{8,9},{9,10},{10,1... | collective-permute-start | bytes 786440 | tf_op jit(solution)/shard_map/ppermute | solution.py:17
  288.9 7.0 %collective-permute-start.2 = (bf16[4,64,512]{2,1,0:T(8,128)(2,1)S(1)}, bf16[4,64,512]{2,1,0:T(8,128)(2,1)S(1)}, u32[]{:S(2)}, u32[]{:S(2)}) collective-permute-start(bf16[4,64,512]{2,1,0:T(8,128)(2,1)S(1)} %collective-permute-done.1), channel_id=1, source_target_pairs={{0,1},{1,2},{2,3},{3,4},{4,5},{5,6},{6,7},{7,0},{8,9},{9,10},{10,1... | collective-permute-start | bytes 786440 | tf_op jit(solution)/shard_map/ppermute | solution.py:17
  295.9 7.0 %collective-permute-start.3 = (bf16[4,64,512]{2,1,0:T(8,128)(2,1)S(1)}, bf16[4,64,512]{2,1,0:T(8,128)(2,1)S(1)}, u32[]{:S(2)}, u32[]{:S(2)}) collective-permute-start(bf16[4,64,512]{2,1,0:T(8,128)(2,1)S(1)} %collective-permute-done.2), channel_id=1, source_target_pairs={{0,1},{1,2},{2,3},{3,4},{4,5},{5,6},{6,7},{7,0},{8,9},{9,10},{10,1... | collective-permute-start | bytes 786440 | tf_op jit(solution)/shard_map/ppermute | solution.py:17
  302.9 7.0 %collective-permute-start.4 = (bf16[4,64,512]{2,1,0:T(8,128)(2,1)S(1)}, bf16[4,64,512]{2,1,0:T(8,128)(2,1)S(1)}, u32[]{:S(2)}, u32[]{:S(2)}) collective-permute-start(bf16[4,64,512]{2,1,0:T(8,128)(2,1)S(1)} %collective-permute-done.3), channel_id=1, source_target_pairs={{0,1},{1,2},{2,3},{3,4},{4,5},{5,6},{6,7},{7,0},{8,9},{9,10},{10,1... | collective-permute-start | bytes 786440 | tf_op jit(solution)/shard_map/ppermute | solution.py:17
  309.9 7.0 %collective-permute-start.5 = (bf16[4,64,512]{2,1,0:T(8,128)(2,1)S(1)}, bf16[4,64,512]{2,1,0:T(8,128)(2,1)S(1)}, u32[]{:S(2)}, u32[]{:S(2)}) collective-permute-start(bf16[4,64,512]{2,1,0:T(8,128)(2,1)S(1)} %collective-permute-done.4), channel_id=1, source_target_pairs={{0,1},{1,2},{2,3},{3,4},{4,5},{5,6},{6,7},{7,0},{8,9},{9,10},{10,1... | collective-permute-start | bytes 786440 | tf_op jit(solution)/shard_map/ppermute | solution.py:17
  316.9 7.0 %collective-permute-start.6 = (bf16[4,64,512]{2,1,0:T(8,128)(2,1)S(1)}, bf16[4,64,512]{2,1,0:T(8,128)(2,1)S(1)}, u32[]{:S(2)}, u32[]{:S(2)}) collective-permute-start(bf16[4,64,512]{2,1,0:T(8,128)(2,1)S(1)} %collective-permute-done.5), channel_id=1, source_target_pairs={{0,1},{1,2},{2,3},{3,4},{4,5},{5,6},{6,7},{7,0},{8,9},{9,10},{10,1... | collective-permute-start | bytes 786440 | tf_op jit(solution)/shard_map/ppermute | solution.py:17
  326.4 3.8 %copy-start = (f32[1,10,64,512]{3,2,1,0:T(8,128)S(1)}, f32[1,10,64,512]{3,2,1,0:T(8,128)}, u32[]{:S(2)}) copy-start(f32[1,10,64,512]{3,2,1,0:T(8,128)} %param.9) | copy-start | bytes 3932164
Sparse Core Ops, SparseCore 0:
  176.2 70.5 all-gather.2
